TPU v7x, 256 devices: a whole 4x4x8 slice. The times are simulated.
256 devices in a mesh: fsdp: 32 (over x_lo, z, core), ctx: 8 (over y, x_hi).
Axes of the slice: x: 4 (x_hi: 2, x_lo: 2; x = x_hi * 2 + x_lo), y: 4, z: 8, core: 2. Of those that a mesh axis runs over, the one named last changes fastest.
Arguments:
- tokens: bfloat16 [32, 4096, 4096], P('fsdp', 'ctx'), may hold values from -24 to 24
- w_query: bfloat16 [4096, 2, 128], P('fsdp'), may hold values from -0.09375 to 0.09375
- w_key: bfloat16 [4096, 2, 128], P('fsdp'), may hold values from -0.09375 to 0.09375
- w_value: bfloat16 [4096, 2, 4, 128], P('fsdp'), may hold values from -0.09375 to 0.09375
- w_out: bfloat16 [2, 4, 128, 4096], P(None, None, None, 'fsdp'), may hold values from -0.5 to 0.5
- value_experts: int32 [32, 4096, 2, 2], P('fsdp', 'ctx'), may hold values from 0 to 3, all different within a row
- value_gates: bfloat16 [32, 4096, 2, 2], P('fsdp', 'ctx'), may hold values from 0.25 to 1
- output_experts: int32 [32, 4096, 2, 2], P('fsdp', 'ctx'), may hold values from 0 to 3, all different within a row
- output_gates: bfloat16 [32, 4096, 2, 2], P('fsdp', 'ctx'), may hold values from 0.25 to 1
Outputs:
- projected: bfloat16 [32, 4096, 4096], P('fsdp', 'ctx')
Inputs may be any that keep to these rules, and one draw needn't show every extreme that they name: `value_experts`: each token and head names 2 different experts. `output_experts`: each token and head names 2 different experts.
All inputs are finite; a program needn't handle non-finite values.
Results may differ from a plain program's by a relative error of at most 0.015.
The roundings to bfloat16 on the way count: a program that leaves them out, or rounds other values in their place, can miss the bound.
Values may be sent and summed in bfloat16 or wider, within the bound.
No kernel may reach another device: no remote copies, remote signals or barrier semaphores. Data moves between devices by JAX's collectives and lax.ppermute only.
A program may use at most 128 MiB of HBM per device.

v0:
```python
import math
import jax
import jax.numpy as jnp
from jax import lax
from jax.sharding import PartitionSpec as P


def passed_along(shard, axis, by):
    count = lax.axis_size(axis)
    pairs = [(i, i + by) for i in range(count) if 0 <= i + by < count]
    return lax.ppermute(shard, axis, pairs)


def expert_mix(indices, gates, experts):
    one_hot = (indices[..., None] == jnp.arange(experts, dtype=jnp.int32)).astype(jnp.float32)
    return jnp.sum(gates.astype(jnp.float32)[..., None] * one_hot, axis=-2)


def attend(totals, queries, key_rows, value_rows, query_pos, key_start):
    run_max, run_sum, run_acc = totals
    scores = jnp.einsum(
        "qhd,khd->hqk", queries, key_rows, preferred_element_type=jnp.float32
    ) / math.sqrt(queries.shape[2])
    key_pos = key_start + jnp.arange(key_rows.shape[0], dtype=jnp.int32)
    visible = (query_pos[:, None] >= key_pos[None, :])[None]
    scores = jnp.where(visible, scores, -jnp.inf)
    new_max = jnp.maximum(run_max, jnp.max(scores, axis=-1))
    rescale = jnp.exp(run_max - new_max)
    weights = jnp.exp(scores - new_max[..., None])
    run_sum = run_sum * rescale + jnp.sum(weights, axis=-1)
    update = jnp.einsum(
        "hqk,khd->qhd", weights.astype(jnp.bfloat16), value_rows, preferred_element_type=jnp.float32
    )
    run_acc = run_acc * jnp.transpose(rescale)[:, :, None] + update
    return (new_max, run_sum, run_acc)


def on_device(
    tokens, w_query, w_key, w_value, w_out, value_experts, value_gates, output_experts, output_gates
):
    tok_rows = tokens.shape[1]
    inputs = tokens[0]
    head_count = w_query.shape[1]
    head_dim = w_query.shape[2]
    experts = w_value.shape[2]
    pieces = (
        lax.all_gather(w_query, "fsdp", axis=0, tiled=True),
        lax.all_gather(w_key, "fsdp", axis=0, tiled=True),
        lax.all_gather(w_value, "fsdp", axis=0, tiled=True),
    )
    piece_rows = pieces[0].shape[0]
    query_sum, key_sum, value_sum = tuple(
        (
            jnp.dot(inputs, panel.reshape(piece_rows, -1), preferred_element_type=jnp.float32)
            for panel in pieces
        )
    )
    queries = query_sum.astype(jnp.bfloat16).reshape(tok_rows, head_count, head_dim)
    key_rows = key_sum.astype(jnp.bfloat16).reshape(tok_rows, head_count, head_dim)
    value_mix = expert_mix(value_experts[0], value_gates[0], experts)
    value_rows = jnp.sum(
        value_mix[..., None] * value_sum.reshape(tok_rows, head_count, experts, head_dim), axis=2
    ).astype(jnp.bfloat16)
    cycle_size = lax.axis_size("ctx")
    cycle_pos = lax.axis_index("ctx")
    query_pos = cycle_pos * tok_rows + jnp.arange(tok_rows, dtype=jnp.int32)
    start_state = (
        jnp.full((head_count, tok_rows), -1e30, jnp.float32),
        jnp.zeros((head_count, tok_rows), jnp.float32),
        jnp.zeros((tok_rows, head_count, head_dim), jnp.float32),
    )
    kv_block = jnp.stack([key_rows, value_rows])
    first_state = attend(
        start_state, queries, key_rows, value_rows, query_pos, cycle_pos * tok_rows
    )

    def cycle_step(passes, bundle):
        totals, moving = bundle
        moving = passed_along(moving, "ctx", 1)
        owner = cycle_pos - passes - 1
        key_start = jnp.where(owner >= 0, owner * tok_rows, cycle_size * tok_rows)
        totals = attend(totals, queries, moving[0], moving[1], query_pos, key_start)
        return (totals, moving)

    final_state, unused_block = lax.fori_loop(
        0, cycle_size - 1, cycle_step, (first_state, kv_block)
    )
    run_max, run_sum, run_acc = final_state
    attended = (run_acc / jnp.transpose(run_sum)[:, :, None]).astype(jnp.bfloat16)
    output_mix = expert_mix(output_experts[0], output_gates[0], experts).astype(jnp.bfloat16)
    mixed_in = (
        output_mix.astype(jnp.float32)[..., None] * attended.astype(jnp.float32)[:, :, None, :]
    ).astype(jnp.bfloat16)
    mixed_flat = mixed_in.reshape(tok_rows, head_count * experts * head_dim)
    panel_piece = lax.all_gather(w_out, "fsdp", axis=3, tiled=True)
    result = jnp.dot(
        mixed_flat,
        panel_piece.reshape(-1, panel_piece.shape[3]),
        preferred_element_type=jnp.float32,
    )
    return result.astype(jnp.bfloat16)[None]


def solution(mesh):
    in_specs = (
        P("fsdp", "ctx", None),
        P("fsdp", None, None),
        P("fsdp", None, None),
        P("fsdp", None, None, None),
        P(None, None, None, "fsdp"),
        P("fsdp", "ctx", None, None),
        P("fsdp", "ctx", None, None),
        P("fsdp", "ctx", None, None),
        P("fsdp", "ctx", None, None),
    )
    out_specs = P("fsdp", "ctx", None)
    return jax.shard_map(
        on_device, mesh=mesh, in_specs=in_specs, out_specs=out_specs, check_vma=False
    )
```

profile of v0, /device:TPU:248, one launch (start us, length us, event | category | flops | bytes accessed | tf_op | source)
XLA Modules:
  0.0 401.1 jit_solution(15075435414131235273)
XLA Ops:
  6.5 0.7 all-gather.7.cloned.1.call-update
  7.3 0.7 all-gather.5.cloned.1.call-update
  8.1 0.7 all-gather.9.cloned.1.call-update
  8.8 0.5 all-gather.11.cloned.1.call-update
  9.3 0.7 bitcast_convert_fusion.2
  10.0 0.7 select_reduce_fusion.1
  10.8 0.7 bitcast_convert_fusion.1
  11.4 0.7 select_reduce_fusion
  12.4 60.2 %all-gather.7.cloned.1.call-done = bf16[4096,2,128]{2,1,0:T(2,128)(2,1)} async-done(((bf16[128,2,128]{2,1,0:T(2,128)(2,1)}), bf16[4096,2,128]{2,1,0:T(2,128)(2,1)}) %all-gather.7.cloned.1.call-update) | async-done | bytes 2097168 | tf_op jit(solution)/shard_map/all_gather | solution.py:48
  72.6 4.2 %fusion.40 = bf16[512,256]{0,1:T(8,128)(2,1)S(1)} fusion(bf16[512,8,2,128]{3,2,1,0:T(2,128)(2,1)} %bitcast.103, bf16[1,512,4096]{2,1,0:T(8,128)(2,1)} %param.11), kind=kOutput, calls=%fused_computation.46 | convolution fusion | flops 1073872896 | bytes 6553600 | tf_op jit(solution)/shard_map/dot_general | solution.py:54
  76.9 61.9 %all-gather.5.cloned.1.call-done = bf16[4096,2,128]{2,1,0:T(2,128)(2,1)} async-done(((bf16[128,2,128]{2,1,0:T(2,128)(2,1)}), bf16[4096,2,128]{2,1,0:T(2,128)(2,1)}) %all-gather.5.cloned.1.call-update) | async-done | bytes 2097168 | tf_op jit(solution)/shard_map/all_gather | solution.py:47
  138.8 4.2 %fusion.35 = bf16[512,256]{0,1:T(8,128)(2,1)S(1)} fusion(bf16[512,8,2,128]{3,2,1,0:T(2,128)(2,1)} %bitcast.104, bf16[1,512,4096]{2,1,0:T(8,128)(2,1)} %param.11), kind=kOutput, calls=%fused_computation.45 | convolution fusion | flops 1073872896 | bytes 6553600 | tf_op jit(solution)/shard_map/dot_general | solution.py:54
  143.2 0.6 fusion.27
  144.3 68.5 %all-gather.9.cloned.1.call-done = bf16[4096,2,4,128]{3,2,1,0:T(4,128)(2,1)} async-done(((bf16[128,2,4,128]{3,2,1,0:T(4,128)(2,1)}), bf16[4096,2,4,128]{3,2,1,0:T(4,128)(2,1)}) %all-gather.9.cloned.1.call-update) | async-done | bytes 8388624 | tf_op jit(solution)/shard_map/all_gather | solution.py:49
  212.8 13.8 %copy.52 = bf16[4096,2,4,128]{0,3,2,1:T(8,128)(2,1)} copy(bf16[4096,2,4,128]{3,2,1,0:T(4,128)(2,1)} %all-gather.9.cloned.1.call-done) | data formatting | bytes 16777216 | tf_op jit(solution)/shard_map/reshape | solution.py:54
  226.7 9.1 %multiply_reduce_fusion = bf16[512,2,128]{2,0,1:T(8,128)(2,1)} fusion(bf16[4096,2,4,128]{0,3,2,1:T(8,128)(2,1)} %copy.52, bf16[1,512,4096]{2,1,0:T(8,128)(2,1)} %param.11, f32[512,2,4]{0,2,1:T(4,128)S(1)} %select_reduce_fusion), kind=kOutput, calls=%fused_computation.37 | convolution fusion | flops 4295884800 | bytes 12861440 | tf_op jit(solution)/shard_map/dot_general | solution.py:54
  235.8 1.7 fusion.34
  237.7 1.0 pad_maximum_fusion
  238.7 147.3 %while.22 = (s32[]{:T(128)}, f32[2,512]{1,0:T(2,128)S(1)}, f32[2,512]{1,0:T(2,128)S(1)}, f32[512,2,128]{2,0,1:T(8,128)S(1)}, bf16[2,512,2,128]{3,1,2,0:T(8,128)(...) while((s32[]{:T(128)}, f32[2,512]{1,0:T(2,128)S(1)}, ...), condition=%wide.region_8.9_spmd.clone, body=%wide.region_5.8_spmd.clone.sunk | while | flops 274731008 | bytes 12394735 | solution.py:85
  238.7 4.9 %collective-permute-start = (bf16[2,512,2,128]{3,1,2,0:T(8,128)(2,1)S(1)}, bf16[2,512,2,128]{3,1,2,0:T(8,128)(2,1)S(1)}, u32[]{:S(2)}, u32[]{:S(2)}) collective-permute-start(bf16[2,512,2,128]{3,1,2,0:T(8,128)(2,1)S(1)} %get-tuple-element.353), channel_id=1, source_target_pairs={{0,1},{1,2},{2,3},{3,4},{4,5},{5,6},{6,7},{8,9},{9,10},{10,11},{11... | collective-permute-start | bytes 1572872 | tf_op jit(solution)/shard_map/while/body/eval_jaxpr/ppermute | solution.py:11
  243.8 22.6 %collective-permute-done = bf16[2,512,2,128]{3,1,2,0:T(8,128)(2,1)S(1)} collective-permute-done((bf16[2,512,2,128]{3,1,2,0:T(8,128)(2,1)S(1)}, bf16[2,512,2,128]{3,1,2,0:T(8,128)(2,1)S(1)}, u32[]{:S(2)}, u32[]{:S(2)}) %collective-permute-start) | collective-permute-done | bytes 524320 | tf_op jit(solution)/shard_map/while/body/eval_jaxpr/ppermute | solution.py:11
  266.5 0.5 fusion.71
  267.6 1.0 fusion.74
  268.6 2.6 collective-permute-start
  271.5 25.0 %collective-permute-done = bf16[2,512,2,128]{3,1,2,0:T(8,128)(2,1)S(1)} collective-permute-done((bf16[2,512,2,128]{3,1,2,0:T(8,128)(2,1)S(1)}, bf16[2,512,2,128]{3,1,2,0:T(8,128)(2,1)S(1)}, u32[]{:S(2)}, u32[]{:S(2)}) %collective-permute-start) | collective-permute-done | bytes 524320 | tf_op jit(solution)/shard_map/while/body/eval_jaxpr/ppermute | solution.py:11
  296.5 0.5 fusion.71
  297.7 1.0 fusion.74
  298.7 2.0 collective-permute-start
  300.9 16.0 %collective-permute-done = bf16[2,512,2,128]{3,1,2,0:T(8,128)(2,1)S(1)} collective-permute-done((bf16[2,512,2,128]{3,1,2,0:T(8,128)(2,1)S(1)}, bf16[2,512,2,128]{3,1,2,0:T(8,128)(2,1)S(1)}, u32[]{:S(2)}, u32[]{:S(2)}) %collective-permute-start) | collective-permute-done | bytes 524320 | tf_op jit(solution)/shard_map/while/body/eval_jaxpr/ppermute | solution.py:11
  316.9 0.5 fusion.71
  318.0 1.0 fusion.74
  319.0 3.4 collective-permute-start
  322.7 12.2 %collective-permute-done = bf16[2,512,2,128]{3,1,2,0:T(8,128)(2,1)S(1)} collective-permute-done((bf16[2,512,2,128]{3,1,2,0:T(8,128)(2,1)S(1)}, bf16[2,512,2,128]{3,1,2,0:T(8,128)(2,1)S(1)}, u32[]{:S(2)}, u32[]{:S(2)}) %collective-permute-start) | collective-permute-done | bytes 524320 | tf_op jit(solution)/shard_map/while/body/eval_jaxpr/ppermute | solution.py:11
  334.9 0.5 fusion.71
  336.1 1.0 fusion.74
  337.0 3.7 collective-permute-start
  341.0 11.0 %collective-permute-done = bf16[2,512,2,128]{3,1,2,0:T(8,128)(2,1)S(1)} collective-permute-done((bf16[2,512,2,128]{3,1,2,0:T(8,128)(2,1)S(1)}, bf16[2,512,2,128]{3,1,2,0:T(8,128)(2,1)S(1)}, u32[]{:S(2)}, u32[]{:S(2)}) %collective-permute-start) | collective-permute-done | bytes 524320 | tf_op jit(solution)/shard_map/while/body/eval_jaxpr/ppermute | solution.py:11
  352.0 0.5 fusion.71
  353.2 1.0 fusion.74
  354.2 4.0 collective-permute-start
  358.4 9.9 %collective-permute-done = bf16[2,512,2,128]{3,1,2,0:T(8,128)(2,1)S(1)} collective-permute-done((bf16[2,512,2,128]{3,1,2,0:T(8,128)(2,1)S(1)}, bf16[2,512,2,128]{3,1,2,0:T(8,128)(2,1)S(1)}, u32[]{:S(2)}, u32[]{:S(2)}) %collective-permute-start) | collective-permute-done | bytes 524320 | tf_op jit(solution)/shard_map/while/body/eval_jaxpr/ppermute | solution.py:11
  368.2 0.5 fusion.71
  369.4 1.0 fusion.74
  370.4 4.2 %collective-permute-start = (bf16[2,512,2,128]{3,1,2,0:T(8,128)(2,1)S(1)}, bf16[2,512,2,128]{3,1,2,0:T(8,128)(2,1)S(1)}, u32[]{:S(2)}, u32[]{:S(2)}) collective-permute-start(bf16[2,512,2,128]{3,1,2,0:T(8,128)(2,1)S(1)} %get-tuple-element.353), channel_id=1, source_target_pairs={{0,1},{1,2},{2,3},{3,4},{4,5},{5,6},{6,7},{8,9},{9,10},{10,11},{11... | collective-permute-start | bytes 1572872 | tf_op jit(solution)/shard_map/while/body/eval_jaxpr/ppermute | solution.py:11
  374.8 9.0 %collective-permute-done = bf16[2,512,2,128]{3,1,2,0:T(8,128)(2,1)S(1)} collective-permute-done((bf16[2,512,2,128]{3,1,2,0:T(8,128)(2,1)S(1)}, bf16[2,512,2,128]{3,1,2,0:T(8,128)(2,1)S(1)}, u32[]{:S(2)}, u32[]{:S(2)}) %collective-permute-start) | collective-permute-done | bytes 524320 | tf_op jit(solution)/shard_map/while/body/eval_jaxpr/ppermute | solution.py:11
  383.8 0.5 fusion.71
  385.0 1.0 fusion.74
  386.2 8.3 %fusion.17 = bf16[1,512,4096]{2,1,0:T(8,128)(2,1)} fusion(bf16[2,4,128,4096]{3,2,1,0:T(8,128)(2,1)} %all-gather.11.cloned.1.call-done, f32[512,2,128]{2,0,1:T(8,128)S(1)} %fusion.52, f32[512,2,4]{0,2,1:T(4,128)S(1)} %convert_element_type.118), kind=kOutput, calls=%fused_computation.26 | convolution fusion | flops 4298113024 | bytes 13123584 | tf_op jit(solution)/shard_map/dot_general | solution.py:96
  (64 shorter events, 7.1 us)
Async XLA Ops:
  6.5 66.0 %all-gather.7.cloned.1.call-start = ((), (), s32[]{:S(2)}) async-start(), calls=%async_computation.1 | async-start | bytes 2162688 | tf_op jit(solution)/shard_map/all_gather | solution.py:48
  7.3 131.6 %all-gather.5.cloned.1.call-start = ((), (), s32[]{:S(2)}) async-start(), calls=%async_computation | async-start | bytes 2162688 | tf_op jit(solution)/shard_map/all_gather | solution.py:47
  8.0 204.8 %all-gather.9.cloned.1.call-start = ((), (), s32[]{:S(2)}) async-start(), calls=%async_computation.2 | async-start | bytes 8650752 | tf_op jit(solution)/shard_map/all_gather | solution.py:49
  8.7 377.5 %all-gather.11.cloned.1.call-start = ((), (), s32[]{:S(2)}) async-start(), calls=%async_computation.3 | async-start | bytes 8650752 | tf_op jit(solution)/shard_map/all_gather | solution.py:95
  238.7 27.8 %collective-permute-start = (bf16[2,512,2,128]{3,1,2,0:T(8,128)(2,1)S(1)}, bf16[2,512,2,128]{3,1,2,0:T(8,128)(2,1)S(1)}, u32[]{:S(2)}, u32[]{:S(2)}) collective-permute-start(bf16[2,512,2,128]{3,1,2,0:T(8,128)(2,1)S(1)} %get-tuple-element.353), channel_id=1, source_target_pairs={{0,1},{1,2},{2,3},{3,4},{4,5},{5,6},{6,7},{8,9},{9,10},{10,11},{11... | collective-permute-start | bytes 1572872 | tf_op jit(solution)/shard_map/while/body/eval_jaxpr/ppermute | solution.py:11
  268.6 27.9 %collective-permute-start = (bf16[2,512,2,128]{3,1,2,0:T(8,128)(2,1)S(1)}, bf16[2,512,2,128]{3,1,2,0:T(8,128)(2,1)S(1)}, u32[]{:S(2)}, u32[]{:S(2)}) collective-permute-start(bf16[2,512,2,128]{3,1,2,0:T(8,128)(2,1)S(1)} %get-tuple-element.353), channel_id=1, source_target_pairs={{0,1},{1,2},{2,3},{3,4},{4,5},{5,6},{6,7},{8,9},{9,10},{10,11},{11... | collective-permute-start | bytes 1572872 | tf_op jit(solution)/shard_map/while/body/eval_jaxpr/ppermute | solution.py:11
  298.7 18.2 %collective-permute-start = (bf16[2,512,2,128]{3,1,2,0:T(8,128)(2,1)S(1)}, bf16[2,512,2,128]{3,1,2,0:T(8,128)(2,1)S(1)}, u32[]{:S(2)}, u32[]{:S(2)}) collective-permute-start(bf16[2,512,2,128]{3,1,2,0:T(8,128)(2,1)S(1)} %get-tuple-element.353), channel_id=1, source_target_pairs={{0,1},{1,2},{2,3},{3,4},{4,5},{5,6},{6,7},{8,9},{9,10},{10,11},{11... | collective-permute-start | bytes 1572872 | tf_op jit(solution)/shard_map/while/body/eval_jaxpr/ppermute | solution.py:11
  319.0 15.9 %collective-permute-start = (bf16[2,512,2,128]{3,1,2,0:T(8,128)(2,1)S(1)}, bf16[2,512,2,128]{3,1,2,0:T(8,128)(2,1)S(1)}, u32[]{:S(2)}, u32[]{:S(2)}) collective-permute-start(bf16[2,512,2,128]{3,1,2,0:T(8,128)(2,1)S(1)} %get-tuple-element.353), channel_id=1, source_target_pairs={{0,1},{1,2},{2,3},{3,4},{4,5},{5,6},{6,7},{8,9},{9,10},{10,11},{11... | collective-permute-start | bytes 1572872 | tf_op jit(solution)/shard_map/while/body/eval_jaxpr/ppermute | solution.py:11
  337.0 15.0 %collective-permute-start = (bf16[2,512,2,128]{3,1,2,0:T(8,128)(2,1)S(1)}, bf16[2,512,2,128]{3,1,2,0:T(8,128)(2,1)S(1)}, u32[]{:S(2)}, u32[]{:S(2)}) collective-permute-start(bf16[2,512,2,128]{3,1,2,0:T(8,128)(2,1)S(1)} %get-tuple-element.353), channel_id=1, source_target_pairs={{0,1},{1,2},{2,3},{3,4},{4,5},{5,6},{6,7},{8,9},{9,10},{10,11},{11... | collective-permute-start | bytes 1572872 | tf_op jit(solution)/shard_map/while/body/eval_jaxpr/ppermute | solution.py:11
  354.2 14.1 %collective-permute-start = (bf16[2,512,2,128]{3,1,2,0:T(8,128)(2,1)S(1)}, bf16[2,512,2,128]{3,1,2,0:T(8,128)(2,1)S(1)}, u32[]{:S(2)}, u32[]{:S(2)}) collective-permute-start(bf16[2,512,2,128]{3,1,2,0:T(8,128)(2,1)S(1)} %get-tuple-element.353), channel_id=1, source_target_pairs={{0,1},{1,2},{2,3},{3,4},{4,5},{5,6},{6,7},{8,9},{9,10},{10,11},{11... | collective-permute-start | bytes 1572872 | tf_op jit(solution)/shard_map/while/body/eval_jaxpr/ppermute | solution.py:11
  370.4 13.5 %collective-permute-start = (bf16[2,512,2,128]{3,1,2,0:T(8,128)(2,1)S(1)}, bf16[2,512,2,128]{3,1,2,0:T(8,128)(2,1)S(1)}, u32[]{:S(2)}, u32[]{:S(2)}) collective-permute-start(bf16[2,512,2,128]{3,1,2,0:T(8,128)(2,1)S(1)} %get-tuple-element.353), channel_id=1, source_target_pairs={{0,1},{1,2},{2,3},{3,4},{4,5},{5,6},{6,7},{8,9},{9,10},{10,11},{11... | collective-permute-start | bytes 1572872 | tf_op jit(solution)/shard_map/while/body/eval_jaxpr/ppermute | solution.py:11
Sparse Core Ops, SparseCore 0:
  9.2 63.2 all-gather.6
  74.4 64.3 all-gather.4
  140.7 72.0 all-gather.8
  214.4 96.4 all-gather.10
where the time goes:
time: 402 us; the launch traced here: 401 us
  waiting for transfers between devices  299 us (74%)
  matrix products  38.6 us (10%)
  starting transfers between devices  25 us (6%)
  local copies, waits for them, and re-layouts  14.6 us (4%)
  between operations  13.2 us (3%)
  other arithmetic  9.98 us (2%)
    ppermute x7, waiting for transfers between devices, passed_along(): return lax.ppermute(shard, axis, pairs)  106 us
    all_gather x1, waiting for transfers between devices, on_device(): lax.all_gather(w_value, 'fsdp', axis=0, tiled=True)  68.5 us
    all_gather x1, waiting for transfers between devices, on_device(): lax.all_gather(w_query, 'fsdp', axis=0, tiled=True)  61.9 us
    all_gather x1, waiting for transfers between devices, on_device(): lax.all_gather(w_key, 'fsdp', axis=0, tiled=True)  60.2 us
    ppermute x7, starting transfers between devices, passed_along(): return lax.ppermute(shard, axis, pairs)  24.9 us
    dot_general x3, matrix products, on_device(): jnp.dot(inputs, panel.reshape(piece_rows, -1), preferred_element_type=jnp...  17.4 us
    reshape x1, local copies, waits for them, and re-layouts, on_device(): panel.reshape(piece_rows, -1)  13.8 us
    dot_general x8, matrix products, attend(): jnp.einsum('hqk,khd->qhd', weights.astype(jnp.bfloat16), value_rows, pref...  8.41 us
  transfers between devices with their start and end apart: 11, of which 10 were waited for; matrix products, arithmetic and copies ran while one was open for 14% of the time, Pallas kernels for 0%

commit v1 on v0

--- a/solution.py
+++ b/solution.py
@@ -44,7 +44,9 @@
     head_dim = w_query.shape[2]
     experts = w_value.shape[2]
     pieces = (
-        lax.all_gather(w_query, "fsdp", axis=0, tiled=True),
+        jnp.concatenate(
+            lax.all_to_all(jnp.stack([w_query] * lax.axis_size("fsdp")), "fsdp", 0, 0), axis=0
+        ),
         lax.all_gather(w_key, "fsdp", axis=0, tiled=True),
         lax.all_gather(w_value, "fsdp", axis=0, tiled=True),
     )

time: 402 us -> 352 us (0.88)
  waiting for transfers between devices: 299 us -> 243 us
  starting transfers between devices: 25 us -> 29.7 us
    all_gather x1 -> x0, waiting for transfers between devices: 61.9 us -> none  [on_device(): lax.all_gather(w_query, 'fsdp', axis=0, tiled=True)]
    all_to_all x0 -> x1, starting transfers between devices: none -> 7.08 us  [on_device(): lax.all_to_all(jnp.stack([w_query] * lax.axis_size('fsdp')), 'fsdp', 0, 0)]
    ppermute x7, waiting for transfers between devices: 106 us -> 110 us  [passed_along(): return lax.ppermute(shard, axis, pairs)]
    all_gather x1, waiting for transfers between devices: 60.2 us -> 64.5 us  [on_device(): lax.all_gather(w_key, 'fsdp', axis=0, tiled=True)]
    another operation x0 -> x1, local copies, waits for them, and re-layouts: none -> 4.05 us  [on_device(): jnp.stack([w_query] * lax.axis_size('fsdp'))]
  transfers between devices with their start and end apart: 11 -> 11, of which waited for: 10 -> 9; matrix products, arithmetic and copies ran while one was open for 14% -> 16% of each run, Pallas kernels for 0% -> 0%
where the time goes in v1:
time: 352 us; the launch traced here: 351 us
  waiting for transfers between devices  243 us (69%)
  matrix products  37.9 us (11%)
  starting transfers between devices  29.7 us (8%)
  local copies, waits for them, and re-layouts  18.6 us (5%)
  between operations  13.3 us (4%)
  other arithmetic  7.22 us (2%)
    ppermute x7, waiting for transfers between devices, passed_along(): return lax.ppermute(shard, axis, pairs)  110 us
    all_gather x1, waiting for transfers between devices, on_device(): lax.all_gather(w_value, 'fsdp', axis=0, tiled=True)  66.3 us
    all_gather x1, waiting for transfers between devices, on_device(): lax.all_gather(w_key, 'fsdp', axis=0, tiled=True)  64.5 us
    ppermute x7, starting transfers between devices, passed_along(): return lax.ppermute(shard, axis, pairs)  22.6 us
    dot_general x3, matrix products, on_device(): jnp.dot(inputs, panel.reshape(piece_rows, -1), preferred_element_type=jnp...  16.8 us
    reshape x1, local copies, waits for them, and re-layouts, on_device(): panel.reshape(piece_rows, -1)  13.8 us
    dot_general x8, matrix products, attend(): jnp.einsum('hqk,khd->qhd', weights.astype(jnp.bfloat16), value_rows, pref...  8.41 us
    dot_general x1, matrix products, on_device(): jnp.dot(mixed_flat, panel_piece.reshape(-1, panel_piece.shape[3]), prefer...  8.32 us
  transfers between devices with their start and end apart: 11, of which 9 were waited for; matrix products, arithmetic and copies ran while one was open for 16% of the time, Pallas kernels for 0%

profile of v1, /device:TPU:248, one launch (start us, length us, event | category | flops | bytes accessed | tf_op | source)
XLA Modules:
  0.0 350.6 jit_solution(2102176849414516956)
XLA Ops:
  6.5 0.7 all-gather.4.cloned.1.call-update
  7.3 0.7 all-gather.6.cloned.1.call-update
  8.0 4.0 %stack.4 = bf16[32,128,2,128]{3,2,1,0:T(2,128)(2,1)} broadcast(bf16[128,2,128]{2,1,0:T(2,128)(2,1)} %param.12), dimensions={1,2,3} | broadcast | bytes 2162688 | tf_op jit(solution)/shard_map/stack | solution.py:48
  12.1 7.1 %all-to-all-start = ((bf16[32,128,2,128]{3,2,1,0:T(2,128)(2,1)}), bf16[32,128,2,128]{3,2,1,0:T(2,128)(2,1)S(1)}, u32[]{:S(2)}, u32[]{:S(2)}) async-start(bf16[32,128,2,128]{3,2,1,0:T(2,128)(2,1)} %stack.4), calls=%async_computation | async-start | bytes 4194304 | tf_op jit(solution)/shard_map/all_to_all | solution.py:48
  19.2 0.7 all-gather.8.cloned.1.call-update
  20.3 64.5 %all-gather.4.cloned.1.call-done = bf16[4096,2,128]{2,1,0:T(2,128)(2,1)} async-done(((bf16[128,2,128]{2,1,0:T(2,128)(2,1)}), bf16[4096,2,128]{2,1,0:T(2,128)(2,1)}) %all-gather.4.cloned.1.call-update) | async-done | bytes 2097168 | tf_op jit(solution)/shard_map/all_gather | solution.py:50
  84.8 4.2 %fusion.40 = bf16[512,256]{0,1:T(8,128)(2,1)S(1)} fusion(bf16[512,8,2,128]{3,2,1,0:T(2,128)(2,1)} %bitcast.105, bf16[1,512,4096]{2,1,0:T(8,128)(2,1)} %param.11), kind=kOutput, calls=%fused_computation.46 | convolution fusion | flops 1073872896 | bytes 6553600 | tf_op jit(solution)/shard_map/dot_general | solution.py:56
  89.1 3.5 fusion.35
  92.8 0.6 fusion.27
  93.4 0.5 fusion.33
  94.0 66.3 %all-gather.6.cloned.1.call-done = bf16[4096,2,4,128]{3,2,1,0:T(4,128)(2,1)} async-done(((bf16[128,2,4,128]{3,2,1,0:T(4,128)(2,1)}), bf16[4096,2,4,128]{3,2,1,0:T(4,128)(2,1)}) %all-gather.6.cloned.1.call-update) | async-done | bytes 8388624 | tf_op jit(solution)/shard_map/all_gather | solution.py:51
  160.3 13.8 %copy.52 = bf16[4096,2,4,128]{0,3,2,1:T(8,128)(2,1)} copy(bf16[4096,2,4,128]{3,2,1,0:T(4,128)(2,1)} %all-gather.6.cloned.1.call-done) | data formatting | bytes 16777216 | tf_op jit(solution)/shard_map/reshape | solution.py:56
  174.1 9.2 %multiply_reduce_fusion = bf16[512,2,128]{2,0,1:T(8,128)(2,1)} fusion(bf16[4096,2,4,128]{0,3,2,1:T(8,128)(2,1)} %copy.52, bf16[1,512,4096]{2,1,0:T(8,128)(2,1)} %param.11, f32[512,2,4]{0,2,1:T(4,128)S(1)} %select_reduce_fusion), kind=kOutput, calls=%fused_computation.37 | convolution fusion | flops 4295884800 | bytes 12861440 | tf_op jit(solution)/shard_map/dot_general | solution.py:56
  183.2 1.7 fusion.34
  185.1 1.0 pad_maximum_fusion
  186.1 149.4 %while.22 = (s32[]{:T(128)}, f32[2,512]{1,0:T(2,128)S(1)}, f32[2,512]{1,0:T(2,128)S(1)}, f32[512,2,128]{2,0,1:T(8,128)S(1)}, bf16[2,512,2,128]{3,1,2,0:T(8,128)(...) while((s32[]{:T(128)}, f32[2,512]{1,0:T(2,128)S(1)}, ...), condition=%wide.region_8.9_spmd.clone, body=%wide.region_5.8_spmd.clone.sunk | while | flops 274731008 | bytes 12394735 | solution.py:87
  186.1 4.9 %collective-permute-start = (bf16[2,512,2,128]{3,1,2,0:T(8,128)(2,1)S(1)}, bf16[2,512,2,128]{3,1,2,0:T(8,128)(2,1)S(1)}, u32[]{:S(2)}, u32[]{:S(2)}) collective-permute-start(bf16[2,512,2,128]{3,1,2,0:T(8,128)(2,1)S(1)} %get-tuple-element.353), channel_id=1, source_target_pairs={{0,1},{1,2},{2,3},{3,4},{4,5},{5,6},{6,7},{8,9},{9,10},{10,11},{11... | collective-permute-start | bytes 1572872 | tf_op jit(solution)/shard_map/while/body/eval_jaxpr/ppermute | solution.py:11
  191.2 21.9 %collective-permute-done = bf16[2,512,2,128]{3,1,2,0:T(8,128)(2,1)S(1)} collective-permute-done((bf16[2,512,2,128]{3,1,2,0:T(8,128)(2,1)S(1)}, bf16[2,512,2,128]{3,1,2,0:T(8,128)(2,1)S(1)}, u32[]{:S(2)}, u32[]{:S(2)}) %collective-permute-start) | collective-permute-done | bytes 524320 | tf_op jit(solution)/shard_map/while/body/eval_jaxpr/ppermute | solution.py:11
  213.1 0.5 fusion.71
  213.7 0.5 fusion.73
  214.2 1.0 fusion.74
  215.2 3.2 collective-permute-start
  218.7 25.2 %collective-permute-done = bf16[2,512,2,128]{3,1,2,0:T(8,128)(2,1)S(1)} collective-permute-done((bf16[2,512,2,128]{3,1,2,0:T(8,128)(2,1)S(1)}, bf16[2,512,2,128]{3,1,2,0:T(8,128)(2,1)S(1)}, u32[]{:S(2)}, u32[]{:S(2)}) %collective-permute-start) | collective-permute-done | bytes 524320 | tf_op jit(solution)/shard_map/while/body/eval_jaxpr/ppermute | solution.py:11
  243.9 0.5 fusion.71
  244.5 0.5 fusion.73
  245.1 1.0 fusion.74
  246.1 2.3 collective-permute-start
  248.6 16.2 %collective-permute-done = bf16[2,512,2,128]{3,1,2,0:T(8,128)(2,1)S(1)} collective-permute-done((bf16[2,512,2,128]{3,1,2,0:T(8,128)(2,1)S(1)}, bf16[2,512,2,128]{3,1,2,0:T(8,128)(2,1)S(1)}, u32[]{:S(2)}, u32[]{:S(2)}) %collective-permute-start) | collective-permute-done | bytes 524320 | tf_op jit(solution)/shard_map/while/body/eval_jaxpr/ppermute | solution.py:11
  264.8 0.5 fusion.71
  265.4 0.5 fusion.73
  265.9 1.0 fusion.74
  266.9 3.2 collective-permute-start
  270.4 12.9 %collective-permute-done = bf16[2,512,2,128]{3,1,2,0:T(8,128)(2,1)S(1)} collective-permute-done((bf16[2,512,2,128]{3,1,2,0:T(8,128)(2,1)S(1)}, bf16[2,512,2,128]{3,1,2,0:T(8,128)(2,1)S(1)}, u32[]{:S(2)}, u32[]{:S(2)}) %collective-permute-start) | collective-permute-done | bytes 524320 | tf_op jit(solution)/shard_map/while/body/eval_jaxpr/ppermute | solution.py:11
  283.3 0.5 fusion.71
  284.5 1.0 fusion.74
  285.5 3.1 collective-permute-start
  288.8 12.1 %collective-permute-done = bf16[2,512,2,128]{3,1,2,0:T(8,128)(2,1)S(1)} collective-permute-done((bf16[2,512,2,128]{3,1,2,0:T(8,128)(2,1)S(1)}, bf16[2,512,2,128]{3,1,2,0:T(8,128)(2,1)S(1)}, u32[]{:S(2)}, u32[]{:S(2)}) %collective-permute-start) | collective-permute-done | bytes 524320 | tf_op jit(solution)/shard_map/while/body/eval_jaxpr/ppermute | solution.py:11
  300.9 0.5 fusion.71
  302.1 1.0 fusion.74
  303.1 3.0 collective-permute-start
  306.3 11.4 %collective-permute-done = bf16[2,512,2,128]{3,1,2,0:T(8,128)(2,1)S(1)} collective-permute-done((bf16[2,512,2,128]{3,1,2,0:T(8,128)(2,1)S(1)}, bf16[2,512,2,128]{3,1,2,0:T(8,128)(2,1)S(1)}, u32[]{:S(2)}, u32[]{:S(2)}) %collective-permute-start) | collective-permute-done | bytes 524320 | tf_op jit(solution)/shard_map/while/body/eval_jaxpr/ppermute | solution.py:11
  317.6 0.5 fusion.71
  318.8 1.0 fusion.74
  319.8 2.8 collective-permute-start
  322.8 10.6 %collective-permute-done = bf16[2,512,2,128]{3,1,2,0:T(8,128)(2,1)S(1)} collective-permute-done((bf16[2,512,2,128]{3,1,2,0:T(8,128)(2,1)S(1)}, bf16[2,512,2,128]{3,1,2,0:T(8,128)(2,1)S(1)}, u32[]{:S(2)}, u32[]{:S(2)}) %collective-permute-start) | collective-permute-done | bytes 524320 | tf_op jit(solution)/shard_map/while/body/eval_jaxpr/ppermute | solution.py:11
  333.4 0.5 fusion.71
  334.5 1.0 fusion.74
  335.8 8.3 %fusion.17 = bf16[1,512,4096]{2,1,0:T(8,128)(2,1)} fusion(bf16[2,4,128,4096]{3,2,1,0:T(8,128)(2,1)} %all-gather.8.cloned.1.call-done, f32[512,2,128]{2,0,1:T(8,128)S(1)} %fusion.52, f32[512,2,4]{0,2,1:T(4,128)S(1)} %convert_element_type.118), kind=kOutput, calls=%fused_computation.26 | convolution fusion | flops 4298113024 | bytes 13123584 | tf_op jit(solution)/shard_map/dot_general | solution.py:98
  (72 shorter events, 5.1 us)
Async XLA Ops:
  6.5 78.2 %all-gather.4.cloned.1.call-start = ((), (), s32[]{:S(2)}) async-start(), calls=%async_computation.1 | async-start | bytes 2162688 | tf_op jit(solution)/shard_map/all_gather | solution.py:50
  7.3 153.0 %all-gather.6.cloned.1.call-start = ((), (), s32[]{:S(2)}) async-start(), calls=%async_computation.2 | async-start | bytes 8650752 | tf_op jit(solution)/shard_map/all_gather | solution.py:51
  12.1 7.8 %copy-start.2 = (bf16[1,512,2,2]{1,3,2,0:T(2,128)(2,1)S(1)}, bf16[1,512,2,2]{1,3,2,0:T(2,128)(2,1)}, u32[]{:S(2)}) copy-start(bf16[1,512,2,2]{1,3,2,0:T(2,128)(2,1)} %param.19) | copy-start | bytes 12292
  12.1 7.9 %copy-start = (s32[1,512,2,2]{1,3,2,0:T(2,128)S(1)}, s32[1,512,2,2]{1,3,2,0:T(2,128)}, u32[]{:S(2)}) copy-start(s32[1,512,2,2]{1,3,2,0:T(2,128)} %param.18) | copy-start | bytes 24580
  12.1 7.9 %copy-start.3 = (bf16[1,512,2,2]{1,3,2,0:T(2,128)(2,1)S(1)}, bf16[1,512,2,2]{1,3,2,0:T(2,128)(2,1)}, u32[]{:S(2)}) copy-start(bf16[1,512,2,2]{1,3,2,0:T(2,128)(2,1)} %param.17) | copy-start | bytes 12292
  12.1 7.9 %copy-start.1 = (s32[1,512,2,2]{1,3,2,0:T(2,128)S(1)}, s32[1,512,2,2]{1,3,2,0:T(2,128)}, u32[]{:S(2)}) copy-start(s32[1,512,2,2]{1,3,2,0:T(2,128)} %param.16) | copy-start | bytes 24580
  12.1 77.1 %all-to-all-start = ((bf16[32,128,2,128]{3,2,1,0:T(2,128)(2,1)}), bf16[32,128,2,128]{3,2,1,0:T(2,128)(2,1)S(1)}, u32[]{:S(2)}, u32[]{:S(2)}) async-start(bf16[32,128,2,128]{3,2,1,0:T(2,128)(2,1)} %stack.4), calls=%async_computation | async-start | bytes 4194304 | tf_op jit(solution)/shard_map/all_to_all | solution.py:48
  19.1 316.6 %all-gather.8.cloned.1.call-start = ((), (), s32[]{:S(2)}) async-start(), calls=%async_computation.3 | async-start | bytes 8650752 | tf_op jit(solution)/shard_map/all_gather | solution.py:97
  186.1 27.0 %collective-permute-start = (bf16[2,512,2,128]{3,1,2,0:T(8,128)(2,1)S(1)}, bf16[2,512,2,128]{3,1,2,0:T(8,128)(2,1)S(1)}, u32[]{:S(2)}, u32[]{:S(2)}) collective-permute-start(bf16[2,512,2,128]{3,1,2,0:T(8,128)(2,1)S(1)} %get-tuple-element.353), channel_id=1, source_target_pairs={{0,1},{1,2},{2,3},{3,4},{4,5},{5,6},{6,7},{8,9},{9,10},{10,11},{11... | collective-permute-start | bytes 1572872 | tf_op jit(solution)/shard_map/while/body/eval_jaxpr/ppermute | solution.py:11
  215.2 28.7 %collective-permute-start = (bf16[2,512,2,128]{3,1,2,0:T(8,128)(2,1)S(1)}, bf16[2,512,2,128]{3,1,2,0:T(8,128)(2,1)S(1)}, u32[]{:S(2)}, u32[]{:S(2)}) collective-permute-start(bf16[2,512,2,128]{3,1,2,0:T(8,128)(2,1)S(1)} %get-tuple-element.353), channel_id=1, source_target_pairs={{0,1},{1,2},{2,3},{3,4},{4,5},{5,6},{6,7},{8,9},{9,10},{10,11},{11... | collective-permute-start | bytes 1572872 | tf_op jit(solution)/shard_map/while/body/eval_jaxpr/ppermute | solution.py:11
  246.1 18.7 %collective-permute-start = (bf16[2,512,2,128]{3,1,2,0:T(8,128)(2,1)S(1)}, bf16[2,512,2,128]{3,1,2,0:T(8,128)(2,1)S(1)}, u32[]{:S(2)}, u32[]{:S(2)}) collective-permute-start(bf16[2,512,2,128]{3,1,2,0:T(8,128)(2,1)S(1)} %get-tuple-element.353), channel_id=1, source_target_pairs={{0,1},{1,2},{2,3},{3,4},{4,5},{5,6},{6,7},{8,9},{9,10},{10,11},{11... | collective-permute-start | bytes 1572872 | tf_op jit(solution)/shard_map/while/body/eval_jaxpr/ppermute | solution.py:11
  266.9 16.4 %collective-permute-start = (bf16[2,512,2,128]{3,1,2,0:T(8,128)(2,1)S(1)}, bf16[2,512,2,128]{3,1,2,0:T(8,128)(2,1)S(1)}, u32[]{:S(2)}, u32[]{:S(2)}) collective-permute-start(bf16[2,512,2,128]{3,1,2,0:T(8,128)(2,1)S(1)} %get-tuple-element.353), channel_id=1, source_target_pairs={{0,1},{1,2},{2,3},{3,4},{4,5},{5,6},{6,7},{8,9},{9,10},{10,11},{11... | collective-permute-start | bytes 1572872 | tf_op jit(solution)/shard_map/while/body/eval_jaxpr/ppermute | solution.py:11
  285.5 15.5 %collective-permute-start = (bf16[2,512,2,128]{3,1,2,0:T(8,128)(2,1)S(1)}, bf16[2,512,2,128]{3,1,2,0:T(8,128)(2,1)S(1)}, u32[]{:S(2)}, u32[]{:S(2)}) collective-permute-start(bf16[2,512,2,128]{3,1,2,0:T(8,128)(2,1)S(1)} %get-tuple-element.353), channel_id=1, source_target_pairs={{0,1},{1,2},{2,3},{3,4},{4,5},{5,6},{6,7},{8,9},{9,10},{10,11},{11... | collective-permute-start | bytes 1572872 | tf_op jit(solution)/shard_map/while/body/eval_jaxpr/ppermute | solution.py:11
  303.1 14.6 %collective-permute-start = (bf16[2,512,2,128]{3,1,2,0:T(8,128)(2,1)S(1)}, bf16[2,512,2,128]{3,1,2,0:T(8,128)(2,1)S(1)}, u32[]{:S(2)}, u32[]{:S(2)}) collective-permute-start(bf16[2,512,2,128]{3,1,2,0:T(8,128)(2,1)S(1)} %get-tuple-element.353), channel_id=1, source_target_pairs={{0,1},{1,2},{2,3},{3,4},{4,5},{5,6},{6,7},{8,9},{9,10},{10,11},{11... | collective-permute-start | bytes 1572872 | tf_op jit(solution)/shard_map/while/body/eval_jaxpr/ppermute | solution.py:11
  319.8 13.6 %collective-permute-start = (bf16[2,512,2,128]{3,1,2,0:T(8,128)(2,1)S(1)}, bf16[2,512,2,128]{3,1,2,0:T(8,128)(2,1)S(1)}, u32[]{:S(2)}, u32[]{:S(2)}) collective-permute-start(bf16[2,512,2,128]{3,1,2,0:T(8,128)(2,1)S(1)} %get-tuple-element.353), channel_id=1, source_target_pairs={{0,1},{1,2},{2,3},{3,4},{4,5},{5,6},{6,7},{8,9},{9,10},{10,11},{11... | collective-permute-start | bytes 1572872 | tf_op jit(solution)/shard_map/while/body/eval_jaxpr/ppermute | solution.py:11
Sparse Core Ops, SparseCore 0:
  9.2 75.5 all-gather.3
  86.6 73.6 all-gather.5
  162.1 96.1 all-gather.7
